TPU v7x, 32 devices: a whole 2x2x4 slice. The times are simulated.
32 devices in a mesh: groups: 2 (over y), seq: 4 (over z), dp: 2 (over x), pair: 2 (over core).
Axes of the slice: x: 2, y: 2, z: 4, core: 2. Of those that a mesh axis runs over, the one named last changes fastest.
Arguments:
- queries: bfloat16 [4, 1024, 2048], P(('groups', 'dp'), ('seq', 'pair')), parts along dimension 0
- key_states: bfloat16 [4, 1024, 2048], P(('groups', 'dp'), ('seq', 'pair')), parts along dimension 0
- value_states: bfloat16 [4, 1024, 2048], P(('groups', 'dp'), ('seq', 'pair')), parts along dimension 0, may hold values from -6 to 6
- grad_output: bfloat16 [4, 1024, 2048], P(('groups', 'dp'), ('seq', 'pair')), parts along dimension 0
- gain_query: float32 [128], replicated, may hold values from 0.1 to 1.9
- gain_key: float32 [128], replicated, may hold values from 0.1 to 1.9
- block_keys: int32 [8, 4], replicated, may hold values from 0 to 7, as said below
- block_counts: int32 [8], replicated, may hold values from 1 to 128, as said below
Outputs:
- grad_query: bfloat16 [4, 1024, 2048], P(('groups', 'dp'), ('seq', 'pair')), parts along dimension 0
- grad_key: bfloat16 [4, 1024, 2048], P(('groups', 'dp'), ('seq', 'pair')), parts along dimension 0
- grad_value: bfloat16 [4, 1024, 2048], P(('groups', 'dp'), ('seq', 'pair')), parts along dimension 0
- grad_gain_query: float32 [256], P('groups'), parts along dimension 0
- grad_gain_key: float32 [256], P('groups'), parts along dimension 0
There are 2 independent parts, one for each index of `groups`. A program takes and returns all parts, laid end to end along the dimension named above; an argument that names none is the same for every part. Nothing has to cross between parts.
Inputs may be any that keep to these rules, and one draw needn't show every extreme that they name: `block_keys`: each query block reads itself first, then three other blocks; the four are distinct. `block_counts`: some block is fully live and some block has one live position.
All inputs are finite; a program needn't handle non-finite values.
Results may differ from a plain program's by a relative error of at most 0.0087.
Values may be sent and summed in bfloat16 or wider, within the bound.
A program may use at most 128 MiB of HBM per device.

v0:
```python
import math

import jax
import jax.numpy as jnp
from jax import lax
from jax.sharding import PartitionSpec as P

BLOCK = 128


EPS = 1e-06


def normalize(states, gain):
    float_states = states.astype(jnp.float32)
    inverse = lax.rsqrt(jnp.mean(float_states * float_states, -1, keepdims=True) + EPS)
    return (float_states, inverse, (float_states * inverse * gain).astype(jnp.bfloat16))


def norm_backward(float_states, inverse, gain, grad_hat):
    grad_float = grad_hat.astype(jnp.float32)
    scaled = grad_float * gain
    inner = jnp.mean(scaled * float_states, -1, keepdims=True)
    grad_states = inverse * scaled - float_states * inverse * inverse * inverse * inner
    return (grad_states, jnp.sum(grad_float * float_states * inverse, axis=(0, 1)))


def to_items(states, row_parts):
    tokens, heads, head_dim = states.shape
    blocks_here = tokens // BLOCK
    shaped = states.reshape(blocks_here, row_parts, BLOCK // row_parts, heads, head_dim)
    return shaped.transpose(3, 1, 0, 2, 4).reshape(
        heads * row_parts, blocks_here, BLOCK // row_parts, head_dim
    )


def from_items(items, heads):
    total, blocks_here, piece_rows, head_dim = items.shape
    shaped = items.reshape(heads, total // heads, blocks_here, piece_rows, head_dim)
    return shaped.transpose(2, 1, 3, 0, 4).reshape(
        blocks_here * (total // heads) * piece_rows, heads, head_dim
    )


def key_copies(states, row_parts):
    tokens, heads, head_dim = states.shape
    shaped = states.reshape(tokens // BLOCK, BLOCK, heads, head_dim).transpose(2, 0, 1, 3)
    return jnp.repeat(shaped, row_parts, axis=0)


def fold_parts(items, heads):
    total, blocks_here, block_rows, head_dim = items.shape
    summed = jnp.sum(
        items.reshape(heads, total // heads, blocks_here, block_rows, head_dim), axis=1
    )
    return (
        summed.astype(jnp.bfloat16)
        .transpose(1, 2, 0, 3)
        .reshape(blocks_here * block_rows, heads, head_dim)
    )


def attend(query_items, grad_items, key_full, value_full, block_keys, block_counts):
    local_heads, total_blocks, piece_rows, head_dim = query_items.shape
    key_slots = block_keys.shape[1]
    group_blocks = max(1, min(total_blocks, 512 // piece_rows))
    while total_blocks % group_blocks:
        group_blocks = group_blocks // 2
    group_count = total_blocks // group_blocks
    score_scale = 1.0 / math.sqrt(head_dim)

    def one_group(turn, carry):
        grad_query, grad_keys, grad_values = carry
        head_at = turn // group_count
        first = turn % group_count * group_blocks
        query_block = lax.dynamic_slice(
            query_items, (head_at, first, 0, 0), (1, group_blocks, piece_rows, head_dim)
        )[0]
        grad_block = lax.dynamic_slice(
            grad_items, (head_at, first, 0, 0), (1, group_blocks, piece_rows, head_dim)
        )[0]
        chosen = lax.dynamic_slice_in_dim(block_keys, first, group_blocks, 0).reshape(-1)
        key_rows = jnp.take(lax.dynamic_index_in_dim(key_full, head_at, 0, False), chosen, axis=0)
        key_rows = key_rows.reshape(group_blocks, key_slots * BLOCK, head_dim)
        value_rows = jnp.take(
            lax.dynamic_index_in_dim(value_full, head_at, 0, False), chosen, axis=0
        )
        value_rows = value_rows.reshape(group_blocks, key_slots * BLOCK, head_dim)
        live_counts = jnp.take(block_counts, chosen).reshape(group_blocks, key_slots, 1)
        live_mask = (
            lax.broadcasted_iota(jnp.int32, (group_blocks, key_slots, BLOCK), 2) < live_counts
        )
        live_mask = live_mask.reshape(group_blocks, 1, key_slots * BLOCK)
        scores = (
            jnp.einsum("nqd,nkd->nqk", query_block, key_rows, preferred_element_type=jnp.float32)
            * score_scale
        )
        expd_scores = jnp.where(live_mask, jnp.exp(scores), 0.0)
        attn_probs = expd_scores / jnp.sum(expd_scores, -1, keepdims=True)
        probs_low = attn_probs.astype(jnp.bfloat16)
        attended = jnp.einsum(
            "nqk,nkd->nqd", probs_low, value_rows, preferred_element_type=jnp.float32
        )
        delta_row = jnp.sum(grad_block.astype(jnp.float32) * attended, -1, keepdims=True)
        d_probs = jnp.einsum(
            "nqd,nkd->nqk", grad_block, value_rows, preferred_element_type=jnp.float32
        )
        d_scores = (attn_probs * (d_probs - delta_row) * score_scale).astype(jnp.bfloat16)
        query_grad = jnp.einsum(
            "nqk,nkd->nqd", d_scores, key_rows, preferred_element_type=jnp.float32
        ).astype(jnp.bfloat16)
        key_terms = jnp.einsum(
            "nqk,nqd->nkd", d_scores, query_block, preferred_element_type=jnp.float32
        )
        value_terms = jnp.einsum(
            "nqk,nqd->nkd", probs_low, grad_block, preferred_element_type=jnp.float32
        )
        key_terms = key_terms.reshape(group_blocks * key_slots, BLOCK, head_dim)
        value_terms = value_terms.reshape(group_blocks * key_slots, BLOCK, head_dim)
        grad_query = lax.dynamic_update_slice(grad_query, query_grad[None], (head_at, first, 0, 0))
        grad_keys = grad_keys.at[head_at, chosen].add(key_terms)
        grad_values = grad_values.at[head_at, chosen].add(value_terms)
        return (grad_query, grad_keys, grad_values)

    initial = (
        jnp.zeros_like(query_items),
        jnp.zeros(key_full.shape, jnp.float32),
        jnp.zeros(value_full.shape, jnp.float32),
    )
    return lax.fori_loop(0, local_heads * group_count, one_group, initial)


def on_device(
    queries, key_states, value_states, grad_output, gain_query, gain_key, block_keys, block_counts
):
    tokens = queries.shape[1]
    head_dim = gain_query.shape[0]
    heads = queries.shape[2] // head_dim
    group_width = lax.axis_size(("seq", "pair"))
    row_parts = max(1, group_width // heads)
    query_float, query_inverse, query_hat = normalize(
        queries[0].reshape(tokens, heads, head_dim), gain_query
    )
    key_float, key_inverse, key_hat = normalize(
        key_states[0].reshape(tokens, heads, head_dim), gain_key
    )
    value_rows = value_states[0].reshape(tokens, heads, head_dim)
    grad_rows = grad_output[0].reshape(tokens, heads, head_dim)
    query_items, grad_items = (
        lax.all_to_all(
            to_items(query_hat, row_parts), ("seq", "pair"), split_axis=0, concat_axis=1, tiled=True
        ),
        lax.all_to_all(
            to_items(grad_rows, row_parts), ("seq", "pair"), split_axis=0, concat_axis=1, tiled=True
        ),
    )
    key_items, value_items = (
        lax.all_to_all(
            key_copies(key_hat, row_parts), ("seq", "pair"), split_axis=0, concat_axis=1, tiled=True
        ),
        lax.all_to_all(
            key_copies(value_rows, row_parts),
            ("seq", "pair"),
            split_axis=0,
            concat_axis=1,
            tiled=True,
        ),
    )
    grad_query_items, grad_keys, grad_values = attend(
        query_items, grad_items, key_items, value_items, block_keys, block_counts
    )
    back_query = lax.all_to_all(
        grad_query_items, ("seq", "pair"), split_axis=1, concat_axis=0, tiled=True
    )
    back_keys, back_values = (
        lax.all_to_all(
            grad_keys.astype(jnp.bfloat16), ("seq", "pair"), split_axis=1, concat_axis=0, tiled=True
        ).astype(grad_keys.dtype),
        lax.all_to_all(
            grad_values.astype(jnp.bfloat16),
            ("seq", "pair"),
            split_axis=1,
            concat_axis=0,
            tiled=True,
        ).astype(grad_values.dtype),
    )
    grad_query_hat = from_items(back_query, heads)
    grad_key_hat = fold_parts(back_keys, heads)
    grad_value_rows = fold_parts(back_values, heads)
    grad_query_rows, query_term = norm_backward(
        query_float, query_inverse, gain_query, grad_query_hat
    )
    grad_key_rows, key_term = norm_backward(key_float, key_inverse, gain_key, grad_key_hat)
    query_total, key_total = lax.psum((query_term, key_term), ("seq", "dp", "pair"))
    out_shape = queries.shape
    return (
        grad_query_rows.astype(jnp.bfloat16).reshape(out_shape),
        grad_key_rows.astype(jnp.bfloat16).reshape(out_shape),
        grad_value_rows.reshape(out_shape),
        query_total,
        key_total,
    )


def solution(mesh):
    placed = (
        P(("groups", "dp"), ("seq", "pair"), None),
        P(("groups", "dp"), ("seq", "pair"), None),
        P(("groups", "dp"), ("seq", "pair"), None),
        P(("groups", "dp"), ("seq", "pair"), None),
        P(),
        P(),
        P(),
        P(),
    )
    return jax.shard_map(
        on_device,
        mesh=mesh,
        in_specs=placed,
        out_specs=(
            P(("groups", "dp"), ("seq", "pair"), None),
            P(("groups", "dp"), ("seq", "pair"), None),
            P(("groups", "dp"), ("seq", "pair"), None),
            P("groups"),
            P("groups"),
        ),
        check_vma=False,
    )
```

profile of v0, /device:TPU:0, one launch (start us, length us, event | category | flops | bytes accessed | tf_op | source)
XLA Modules:
  0.0 240.0 jit_solution(1694236836150996337)
XLA Ops:
  0.6 1.3 copy.62
  2.9 0.9 copy-done.2
  3.7 1.0 fusion.48
  4.7 6.5 %all-to-all-start = ((bf16[16,1,128,128]{2,3,1,0:T(8,128)(2,1)}), bf16[16,1,128,128]{2,3,1,0:T(8,128)(2,1)S(1)}, u32[]{:S(2)}, u32[]{:S(2)}) async-start(bf16[16,1,128,128]{2,3,1,0:T(8,128)(2,1)} %fusion.48), calls=%async_computation | async-start | bytes 1048576 | tf_op jit(solution)/shard_map/all_to_all | solution.py:150
  12.4 0.9 copy-done.4
  13.3 1.0 fusion.49
  14.3 12.2 %all-to-all-done = bf16[16,1,128,128]{2,3,1,0:T(8,128)(2,1)S(1)} async-done(((bf16[16,1,128,128]{2,3,1,0:T(8,128)(2,1)}), bf16[16,1,128,128]{2,3,1,0:T(8,128)(2,1)S(1)}, u32[]{:S(2)}, u32[]{:S(2)}) %all-to-all-start) | async-done | bytes 524320 | tf_op jit(solution)/shard_map/all_to_all | solution.py:150
  26.5 0.8 copy-done.11
  27.3 4.2 %all-to-all-start.1 = ((bf16[16,1,128,128]{2,3,1,0:T(8,128)(2,1)}), bf16[16,1,128,128]{2,3,1,0:T(8,128)(2,1)}, u32[]{:S(2)}, u32[]{:S(2)}) async-start(bf16[16,1,128,128]{2,3,1,0:T(8,128)(2,1)} %fusion.49), calls=%async_computation.1 | async-start | bytes 1048576 | tf_op jit(solution)/shard_map/all_to_all | solution.py:158
  31.5 1.0 copy.68
  32.5 14.3 %all-to-all-done.1 = bf16[16,1,128,128]{2,3,1,0:T(8,128)(2,1)} async-done(((bf16[16,1,128,128]{2,3,1,0:T(8,128)(2,1)}), bf16[16,1,128,128]{2,3,1,0:T(8,128)(2,1)}, u32[]{:S(2)}, u32[]{:S(2)}) %all-to-all-start.1) | async-done | bytes 524320 | tf_op jit(solution)/shard_map/all_to_all | solution.py:158
  46.9 3.6 %all-to-all-start.2 = ((bf16[16,1,128,128]{2,3,1,0:T(8,128)(2,1)}), bf16[16,1,128,128]{2,3,1,0:T(8,128)(2,1)S(1)}, u32[]{:S(2)}, u32[]{:S(2)}) async-start(bf16[16,1,128,128]{2,3,1,0:T(8,128)(2,1)} %bitcast.33), calls=%async_computation.2 | async-start | bytes 1048576 | tf_op jit(solution)/shard_map/all_to_all | solution.py:153
  50.5 1.0 copy.71
  51.5 14.3 %all-to-all-done.2 = bf16[16,1,128,128]{2,3,1,0:T(8,128)(2,1)S(1)} async-done(((bf16[16,1,128,128]{2,3,1,0:T(8,128)(2,1)}), bf16[16,1,128,128]{2,3,1,0:T(8,128)(2,1)S(1)}, u32[]{:S(2)}, u32[]{:S(2)}) %all-to-all-start.2) | async-done | bytes 524320 | tf_op jit(solution)/shard_map/all_to_all | solution.py:153
  65.8 0.8 copy-done.12
  66.6 4.2 %all-to-all-start.3 = ((bf16[16,1,128,128]{2,3,1,0:T(8,128)(2,1)}), bf16[16,1,128,128]{2,3,1,0:T(8,128)(2,1)}, u32[]{:S(2)}, u32[]{:S(2)}) async-start(bf16[16,1,128,128]{2,3,1,0:T(8,128)(2,1)} %bitcast.40), calls=%async_computation.3 | async-start | bytes 1048576 | tf_op jit(solution)/shard_map/all_to_all | solution.py:161
  70.7 15.4 %all-to-all-done.3 = bf16[16,1,128,128]{2,3,1,0:T(8,128)(2,1)} async-done(((bf16[16,1,128,128]{2,3,1,0:T(8,128)(2,1)}), bf16[16,1,128,128]{2,3,1,0:T(8,128)(2,1)}, u32[]{:S(2)}, u32[]{:S(2)}) %all-to-all-start.3) | async-done | bytes 524320 | tf_op jit(solution)/shard_map/all_to_all | solution.py:161
  86.1 0.9 broadcast_in_dim.83.clone
  87.1 1.1 broadcast.270.clone
  88.2 60.6 %while.19 = (s32[]{:T(128)}, bf16[2,8,128,128]{3,2,0,1:T(8,128)(2,1)}, f32[2,8,128,128]{3,2,1,0:T(8,128)S(1)}, f32[2,8,128,128]{3,2,1,0:T(8,128)}, s32[8,4]{0,1:...) while((s32[]{:T(128)}, ...), condition=%wide.region_7.9_spmd, body=%wide.region_2.8_spmd.sunk | while | flops 406328224 | bytes 23894416 | solution.py:130
  88.2 1.1 constant_dynamic-slice_fusion.7
  92.4 1.4 fusion.88
  93.8 0.9 constant_dynamic-slice_fusion.9
  95.6 0.9 fusion.91
  96.6 1.2 fusion.92
  97.8 1.7 scatter_fusion
  99.9 3.4 %scatter_fusion.1 = f32[2,8,128,128]{3,2,1,0:T(8,128)} fusion(f32[2,8,128,128]{3,2,1,0:T(8,128)} %get-tuple-element.432, s32[16]{0:T(128)S(1)} %get-tuple-element.412, f32[16,128,128]{2,1,0:T(8,128)S(1)} %bitcast.234), kind=kCustom, calls=%fused_computation.4.clone.1 | custom fusion | flops 262144 | bytes 3145856 | tf_op jit(solution)/shard_map/while/body/eval_jaxpr/scatter-add | solution.py:122
  103.3 1.1 constant_dynamic-slice_fusion.7
  107.5 1.4 fusion.88
  108.9 0.9 constant_dynamic-slice_fusion.9
  110.7 0.9 fusion.91
  111.7 1.2 fusion.92
  112.9 1.7 scatter_fusion
  115.0 3.4 %scatter_fusion.1 = f32[2,8,128,128]{3,2,1,0:T(8,128)} fusion(f32[2,8,128,128]{3,2,1,0:T(8,128)} %get-tuple-element.432, s32[16]{0:T(128)S(1)} %get-tuple-element.412, f32[16,128,128]{2,1,0:T(8,128)S(1)} %bitcast.234), kind=kCustom, calls=%fused_computation.4.clone.1 | custom fusion | flops 262144 | bytes 3145856 | tf_op jit(solution)/shard_map/while/body/eval_jaxpr/scatter-add | solution.py:122
  118.4 1.1 constant_dynamic-slice_fusion.7
  122.6 1.4 fusion.88
  124.0 0.9 constant_dynamic-slice_fusion.9
  125.8 1.0 fusion.91
  126.8 1.3 fusion.92
  128.0 1.7 scatter_fusion
  130.1 3.4 %scatter_fusion.1 = f32[2,8,128,128]{3,2,1,0:T(8,128)} fusion(f32[2,8,128,128]{3,2,1,0:T(8,128)} %get-tuple-element.432, s32[16]{0:T(128)S(1)} %get-tuple-element.412, f32[16,128,128]{2,1,0:T(8,128)S(1)} %bitcast.234), kind=kCustom, calls=%fused_computation.4.clone.1 | custom fusion | flops 262144 | bytes 3145856 | tf_op jit(solution)/shard_map/while/body/eval_jaxpr/scatter-add | solution.py:122
  133.6 1.1 constant_dynamic-slice_fusion.7
  137.7 1.4 fusion.88
  139.2 0.9 constant_dynamic-slice_fusion.9
  141.0 1.0 fusion.91
  141.9 1.3 fusion.92
  143.2 1.7 scatter_fusion
  145.3 3.5 %scatter_fusion.1 = f32[2,8,128,128]{3,2,1,0:T(8,128)} fusion(f32[2,8,128,128]{3,2,1,0:T(8,128)} %get-tuple-element.432, s32[16]{0:T(128)S(1)} %get-tuple-element.412, f32[16,128,128]{2,1,0:T(8,128)S(1)} %bitcast.234), kind=kCustom, calls=%fused_computation.4.clone.1 | custom fusion | flops 262144 | bytes 3145856 | tf_op jit(solution)/shard_map/while/body/eval_jaxpr/scatter-add | solution.py:122
  148.8 3.5 %all-to-all-start.4 = ((bf16[2,8,128,128]{3,2,0,1:T(8,128)(2,1)}), bf16[2,8,128,128]{3,2,0,1:T(8,128)(2,1)S(1)}, u32[]{:S(2)}, u32[]{:S(2)}) async-start(bf16[2,8,128,128]{3,2,0,1:T(8,128)(2,1)} %get-tuple-element.253), calls=%async_computation.4 | async-start | bytes 1048576 | tf_op jit(solution)/shard_map/all_to_all | solution.py:172
  152.3 0.9 copy.108
  153.2 14.4 %all-to-all-done.4 = bf16[2,8,128,128]{3,2,0,1:T(8,128)(2,1)S(1)} async-done(((bf16[2,8,128,128]{3,2,0,1:T(8,128)(2,1)}), bf16[2,8,128,128]{3,2,0,1:T(8,128)(2,1)S(1)}, u32[]{:S(2)}, u32[]{:S(2)}) %all-to-all-start.4) | async-done | bytes 524320 | tf_op jit(solution)/shard_map/all_to_all | solution.py:172
  167.6 3.5 %all-to-all-start.5 = ((bf16[2,8,128,128]{3,2,0,1:T(8,128)(2,1)}), bf16[2,8,128,128]{3,2,0,1:T(8,128)(2,1)S(1)}, u32[]{:S(2)}, u32[]{:S(2)}) async-start(bf16[2,8,128,128]{3,2,0,1:T(8,128)(2,1)} %copy.108), calls=%async_computation.5 | async-start | bytes 1048576 | tf_op jit(solution)/shard_map/all_to_all | solution.py:176
  171.1 0.9 copy.107
  172.4 13.9 %all-to-all-done.5 = bf16[2,8,128,128]{3,2,0,1:T(8,128)(2,1)S(1)} async-done(((bf16[2,8,128,128]{3,2,0,1:T(8,128)(2,1)}), bf16[2,8,128,128]{3,2,0,1:T(8,128)(2,1)S(1)}, u32[]{:S(2)}, u32[]{:S(2)}) %all-to-all-start.5) | async-done | bytes 524320 | tf_op jit(solution)/shard_map/all_to_all | solution.py:176
  186.4 4.2 %all-to-all-start.6 = ((bf16[2,8,128,128]{3,2,0,1:T(8,128)(2,1)}), bf16[2,8,128,128]{3,2,0,1:T(8,128)(2,1)}, u32[]{:S(2)}, u32[]{:S(2)}) async-start(bf16[2,8,128,128]{3,2,0,1:T(8,128)(2,1)} %copy.107), calls=%async_computation.6 | async-start | bytes 1048576 | tf_op jit(solution)/shard_map/all_to_all | solution.py:179
  190.5 1.1 bitcast_convert_fusion
  191.6 2.7 %copy.82 = f32[16,1,128,128]{2,3,0,1:T(8,128)} copy(f32[16,1,128,128]{3,2,0,1:T(8,128)} %bitcast.246) | data formatting | bytes 2097152 | tf_op jit(solution)/shard_map/convert_element_type | solution.py:21
  194.3 2.0 fusion.43
  196.7 1.0 copy.85
  198.5 1.0 copy.86
  199.5 6.3 %all-to-all-done.6 = bf16[2,8,128,128]{3,2,0,1:T(8,128)(2,1)} async-done(((bf16[2,8,128,128]{3,2,0,1:T(8,128)(2,1)}), bf16[2,8,128,128]{3,2,0,1:T(8,128)(2,1)}, u32[]{:S(2)}, u32[]{:S(2)}) %all-to-all-start.6) | async-done | bytes 524320 | tf_op jit(solution)/shard_map/all_to_all | solution.py:179
  205.9 1.3 copy.84
  207.2 1.0 copy.87
  208.2 31.8 %all-reduce.1 = (f32[128]{0:T(128)}, f32[128]{0:T(128)}) all-reduce(f32[128]{0:T(128)S(1)} %get-tuple-element.339, f32[128]{0:T(128)S(1)} %get-tuple-element.306), channel_id=1, replica_groups=mesh['groups'=2,'seq'=4,'dp'=2,'pair'=2] {'seq','dp','pair'}, use_global_device_ids=true, to_apply=%region_11.13 | all-reduce | flops 256 | bytes 2048 | tf_op jit(solution)/shard_map/psum | solution.py:194
  (146 shorter events, 20.8 us)
Async XLA Ops:
  1.9 0.8 copy-start.7
  2.8 1.0 copy-start.2
  2.9 0.9 copy-start.17
  4.7 6.5 %copy-start.13 = (bf16[1,128,2048]{2,1,0:T(8,128)(2,1)S(1)}, bf16[1,128,2048]{2,1,0:T(8,128)(2,1)}, u32[]{:S(2)}) copy-start(bf16[1,128,2048]{2,1,0:T(8,128)(2,1)} %param.13) | copy-start | bytes 1572868
  4.7 21.8 %all-to-all-start = ((bf16[16,1,128,128]{2,3,1,0:T(8,128)(2,1)}), bf16[16,1,128,128]{2,3,1,0:T(8,128)(2,1)S(1)}, u32[]{:S(2)}, u32[]{:S(2)}) async-start(bf16[16,1,128,128]{2,3,1,0:T(8,128)(2,1)} %fusion.48), calls=%async_computation | async-start | bytes 1048576 | tf_op jit(solution)/shard_map/all_to_all | solution.py:150
  11.5 0.8 copy-start.9
  12.3 1.0 copy-start.4
  12.4 0.9 copy-start.18
  14.3 17.2 %copy-start.14 = (bf16[1,128,2048]{2,1,0:T(8,128)(2,1)S(1)}, bf16[1,128,2048]{2,1,0:T(8,128)(2,1)}, u32[]{:S(2)}) copy-start(bf16[1,128,2048]{2,1,0:T(8,128)(2,1)} %param.15) | copy-start | bytes 1572868
  26.5 0.8 copy-start.11
  27.3 19.5 %all-to-all-start.1 = ((bf16[16,1,128,128]{2,3,1,0:T(8,128)(2,1)}), bf16[16,1,128,128]{2,3,1,0:T(8,128)(2,1)}, u32[]{:S(2)}, u32[]{:S(2)}) async-start(bf16[16,1,128,128]{2,3,1,0:T(8,128)(2,1)} %fusion.49), calls=%async_computation.1 | async-start | bytes 1048576 | tf_op jit(solution)/shard_map/all_to_all | solution.py:158
  46.9 3.6 %copy-start.15 = (bf16[1,128,2048]{2,1,0:T(8,128)(2,1)S(1)}, bf16[1,128,2048]{2,1,0:T(8,128)(2,1)}, u32[]{:S(2)}) copy-start(bf16[1,128,2048]{2,1,0:T(8,128)(2,1)} %param.14) | copy-start | bytes 1572868
  46.9 18.9 %all-to-all-start.2 = ((bf16[16,1,128,128]{2,3,1,0:T(8,128)(2,1)}), bf16[16,1,128,128]{2,3,1,0:T(8,128)(2,1)S(1)}, u32[]{:S(2)}, u32[]{:S(2)}) async-start(bf16[16,1,128,128]{2,3,1,0:T(8,128)(2,1)} %bitcast.33), calls=%async_computation.2 | async-start | bytes 1048576 | tf_op jit(solution)/shard_map/all_to_all | solution.py:153
  65.8 0.8 copy-start.12
  66.6 19.5 %all-to-all-start.3 = ((bf16[16,1,128,128]{2,3,1,0:T(8,128)(2,1)}), bf16[16,1,128,128]{2,3,1,0:T(8,128)(2,1)}, u32[]{:S(2)}, u32[]{:S(2)}) async-start(bf16[16,1,128,128]{2,3,1,0:T(8,128)(2,1)} %bitcast.40), calls=%async_computation.3 | async-start | bytes 1048576 | tf_op jit(solution)/shard_map/all_to_all | solution.py:161
  87.1 1.1 copy-start
  87.1 1.1 copy-start.16
  148.8 18.8 %all-to-all-start.4 = ((bf16[2,8,128,128]{3,2,0,1:T(8,128)(2,1)}), bf16[2,8,128,128]{3,2,0,1:T(8,128)(2,1)S(1)}, u32[]{:S(2)}, u32[]{:S(2)}) async-start(bf16[2,8,128,128]{3,2,0,1:T(8,128)(2,1)} %get-tuple-element.253), calls=%async_computation.4 | async-start | bytes 1048576 | tf_op jit(solution)/shard_map/all_to_all | solution.py:172
  152.3 18.8 %copy-start.1 = (f32[2,8,128,128]{3,2,1,0:T(8,128)S(1)}, f32[2,8,128,128]{3,2,1,0:T(8,128)}, u32[]{:S(2)}) copy-start(f32[2,8,128,128]{3,2,1,0:T(8,128)} %get-tuple-element.255) | copy-start | bytes 3145732
  167.6 18.8 %all-to-all-start.5 = ((bf16[2,8,128,128]{3,2,0,1:T(8,128)(2,1)}), bf16[2,8,128,128]{3,2,0,1:T(8,128)(2,1)S(1)}, u32[]{:S(2)}, u32[]{:S(2)}) async-start(bf16[2,8,128,128]{3,2,0,1:T(8,128)(2,1)} %copy.108), calls=%async_computation.5 | async-start | bytes 1048576 | tf_op jit(solution)/shard_map/all_to_all | solution.py:176
  186.4 19.5 %all-to-all-start.6 = ((bf16[2,8,128,128]{3,2,0,1:T(8,128)(2,1)}), bf16[2,8,128,128]{3,2,0,1:T(8,128)(2,1)}, u32[]{:S(2)}, u32[]{:S(2)}) async-start(bf16[2,8,128,128]{3,2,0,1:T(8,128)(2,1)} %copy.107), calls=%async_computation.6 | async-start | bytes 1048576 | tf_op jit(solution)/shard_map/all_to_all | solution.py:179
  191.6 2.7 %copy-start.3 = (f32[1,128,2048]{1,2,0:T(8,128)S(1)}, f32[1,128,2048]{1,2,0:T(8,128)}, u32[]{:S(2)}) copy-start(f32[1,128,2048]{1,2,0:T(8,128)} %copy-done.2) | copy-start | bytes 3145732
  191.6 2.7 %copy-start.5 = (f32[1,128,2048]{1,2,0:T(8,128)S(1)}, f32[1,128,2048]{1,2,0:T(8,128)}, u32[]{:S(2)}) copy-start(f32[1,128,2048]{1,2,0:T(8,128)} %copy-done.4) | copy-start | bytes 3145732
  194.3 2.0 copy-start.8
  196.3 1.4 copy-start.10
  196.7 1.5 copy-start.6
where the time goes:
time: 241 us; the launch traced here: 240 us
  waiting for transfers between devices  90.8 us (38%)
  local copies, waits for them, and re-layouts  40 us (17%)
  blocking collectives  31.8 us (13%)
  starting transfers between devices  29.5 us (12%)
  other arithmetic  27.7 us (11%)
  matrix products  18.7 us (8%)
    psum x1, blocking collectives, on_device(): lax.psum((query_term, key_term), ('seq', 'dp', 'pair'))  31.8 us
    all_to_all x1, waiting for transfers between devices, on_device(): lax.all_to_all(key_copies(value_rows, row_parts), ('seq', 'pair'), split_...  15.4 us
    all_to_all x1, waiting for transfers between devices, on_device(): lax.all_to_all(grad_query_items, ('seq', 'pair'), split_axis=1, concat_ax...  14.4 us
    all_to_all x1, waiting for transfers between devices, on_device(): lax.all_to_all(key_copies(key_hat, row_parts), ('seq', 'pair'), split_axi...  14.3 us
    all_to_all x1, waiting for transfers between devices, on_device(): lax.all_to_all(to_items(grad_rows, row_parts), ('seq', 'pair'), split_axi...  14.3 us
    all_to_all x1, waiting for transfers between devices, on_device(): lax.all_to_all(grad_keys.astype(jnp.bfloat16), ('seq', 'pair'), split_axi...  13.9 us
    scatter-add x4, other arithmetic, one_group(): grad_values = grad_values.at[head_at, chosen].add(value_terms)  13.8 us
    all_to_all x1, waiting for transfers between devices, on_device(): lax.all_to_all(to_items(query_hat, row_parts), ('seq', 'pair'), split_axi...  12.2 us
  transfers between devices with their start and end apart: 7, of which 7 were waited for; matrix products, arithmetic and copies ran while one was open for 6% of the time, Pallas kernels for 0%

commit v1 on v0

--- a/solution.py
+++ b/solution.py
@@ -1,8 +1,11 @@
+import functools
 import math
 
 import jax
 import jax.numpy as jnp
 from jax import lax
+from jax.experimental import pallas as pl
+from jax.experimental.pallas import tpu as pltpu
 from jax.sharding import PartitionSpec as P
 
 BLOCK = 128
@@ -202,6 +205,344 @@
     )
 
 
+MESH = pl.DeviceIdType.MESH
+CHUNK = 256
+LOG2E = 1.4426950408889634
+
+
+def contract_last(left, right):
+    return lax.dot_general(
+        left, right, (((1,), (1,)), ((), ())), preferred_element_type=jnp.float32
+    )
+
+
+def contract(left, right):
+    return jnp.dot(left, right, preferred_element_type=jnp.float32)
+
+
+def fused_kernel(
+    sizes,
+    q_ref, k_ref, v_ref, g_ref, gain_q_ref, gain_k_ref, keys_ref, counts_ref,
+    out_q, out_k, out_v, total_q, total_k,
+    sent, held, bias, acc_k, acc_v, flipped, result, back, gains, gain_held,
+    sent_send, sent_recv, result_send, result_recv, gain_send, gain_recv,
+):
+    pairs, group, replicas, local_heads = sizes
+    tokens = q_ref.shape[0]
+    seq_len = held.shape[2]
+    total_blocks, slots = keys_ref.shape
+    everyone = group * replicas
+    me = lax.axis_index("seq") * pairs + lax.axis_index("pair")
+    me_all = lax.axis_index("dp") * group + me
+
+    def place(index):
+        return {"seq": index // pairs, "pair": index % pairs}
+
+    def place_all(index):
+        inside = index % group
+        return {"dp": index // group, "seq": inside // pairs, "pair": inside % pairs}
+
+    def offset(turn):
+        return group // 2 + ((turn + 1) // 2) * (1 - 2 * (turn % 2))
+
+    barrier = pltpu.get_barrier_semaphore()
+    for step in range(1, everyone):
+        pl.semaphore_signal(
+            barrier, inc=1, device_id=place_all((me_all + step) % everyone), device_id_type=MESH
+        )
+    gain_q = gain_q_ref[...]
+    gain_k = gain_k_ref[...]
+
+    def columns(head):
+        return pl.ds(pl.multiple_of(head * 128, 128), 128)
+
+    def rows(index):
+        return pl.ds(pl.multiple_of(index * tokens, tokens), tokens)
+
+    def inverse_of(states):
+        return lax.rsqrt(jnp.mean(states * states, -1, keepdims=True) + EPS)
+
+    def hat(states, gain):
+        states = states.astype(jnp.float32)
+        return (states * inverse_of(states) * gain).astype(jnp.bfloat16)
+
+    def send_copy(local, turn):
+        peer = (me + offset(turn)) % group
+        return pltpu.make_async_remote_copy(
+            src_ref=sent.at[local, peer],
+            dst_ref=held.at[local, :, rows(me), :],
+            send_sem=sent_send.at[local, turn],
+            recv_sem=sent_recv.at[local, turn],
+            device_id=place(peer),
+            device_id_type=MESH,
+        )
+
+    def arrival(local, turn):
+        source = (me + group - offset(turn)) % group
+        return pltpu.make_async_remote_copy(
+            src_ref=sent.at[local, source],
+            dst_ref=held.at[local, :, rows(source), :],
+            send_sem=sent_send.at[local, turn],
+            recv_sem=sent_recv.at[local, turn],
+            device_id=place(source),
+            device_id_type=MESH,
+        )
+
+    def back_copy(local, turn):
+        peer = (me + offset(turn)) % group
+        return pltpu.make_async_remote_copy(
+            src_ref=result.at[local, :, rows(peer), :],
+            dst_ref=back.at[local, me],
+            send_sem=result_send.at[local, turn],
+            recv_sem=result_recv.at[local, turn],
+            device_id=place(peer),
+            device_id_type=MESH,
+        )
+
+    def back_arrival(local, turn):
+        source = (me + group - offset(turn)) % group
+        return pltpu.make_async_remote_copy(
+            src_ref=result.at[local, :, rows(source), :],
+            dst_ref=back.at[local, source],
+            send_sem=result_send.at[local, turn],
+            recv_sem=result_recv.at[local, turn],
+            device_id=place(source),
+            device_id_type=MESH,
+        )
+
+    for local in range(local_heads):
+
+        def prepare(turn, carry, local=local):
+            peer = (me + offset(turn)) % group
+            at = columns(peer * local_heads + local)
+            sent[local, peer, 0] = hat(q_ref[:, at], gain_q)
+            sent[local, peer, 1] = hat(k_ref[:, at], gain_k)
+            sent[local, peer, 2] = v_ref[:, at]
+            sent[local, peer, 3] = g_ref[:, at]
+            return carry
+
+        def begin(turn, carry, local=local):
+            carry = prepare(turn, carry, local)
+            send_copy(local, turn).start()
+            return carry
+
+        if local == 0:
+            prepare(0, 0)
+            pl.semaphore_wait(barrier, everyone - 1)
+            send_copy(0, 0).start()
+            lax.fori_loop(1, group - 1, begin, 0)
+        else:
+            lax.fori_loop(0, group - 1, begin, 0)
+    for local in range(local_heads):
+        at = columns(me * local_heads + local)
+        held[local, 0, rows(me), :] = hat(q_ref[:, at], gain_q)
+        held[local, 1, rows(me), :] = hat(k_ref[:, at], gain_k)
+        held[local, 2, rows(me), :] = v_ref[:, at]
+        held[local, 3, rows(me), :] = g_ref[:, at]
+
+    place_in = lax.broadcasted_iota(jnp.int32, (BLOCK, BLOCK), 0)
+    for block in range(total_blocks):
+        chunk, side = block // (CHUNK // BLOCK), block % (CHUNK // BLOCK)
+        for other in range(total_blocks):
+            live = counts_ref[other]
+            limit = jnp.int32(0)
+            for slot in range(slots):
+                limit = jnp.where(keys_ref[block, slot] == other, live, limit)
+            bias[
+                chunk, other * BLOCK : (other + 1) * BLOCK, side * BLOCK : (side + 1) * BLOCK
+            ] = jnp.where(place_in < limit, 0.0, -1e30)
+
+    scale = 1.0 / math.sqrt(128)
+    for local in range(local_heads):
+
+        def landed(turn, carry, local=local):
+            arrival(local, turn).wait_recv()
+            return carry
+
+        lax.fori_loop(0, group - 1, landed, 0)
+        keys = held[local, 1]
+        values = held[local, 2]
+        flipped[0] = keys.T
+        flipped[1] = values.T
+        acc_k[...] = jnp.zeros_like(acc_k)
+        acc_v[...] = jnp.zeros_like(acc_v)
+
+        def one_chunk(chunk, carry, local=local):
+            at = pl.ds(pl.multiple_of(chunk * CHUNK, CHUNK), CHUNK)
+            query = held[local, 0, at, :]
+            grad = held[local, 3, at, :]
+            scores = contract_last(held[local, 1], query)
+            expd = jnp.exp2(scores * (scale * LOG2E) + bias[chunk])
+            probs = expd * (1.0 / jnp.sum(expd, 0, keepdims=True))
+            probs_low = probs.astype(jnp.bfloat16)
+            d_probs = contract_last(held[local, 2], grad)
+            attended = contract(flipped[1], probs_low)
+            delta = jnp.sum(grad.T.astype(jnp.float32) * attended, 0, keepdims=True)
+            d_scores = (probs * ((d_probs - delta) * scale)).astype(jnp.bfloat16)
+            grad_query = contract(flipped[0], d_scores)
+            result[local, 0, at, :] = grad_query.T.astype(jnp.bfloat16)
+            acc_k[...] += contract(d_scores, query)
+            acc_v[...] += contract(probs_low, grad)
+            return carry
+
+        lax.fori_loop(0, seq_len // CHUNK, one_chunk, 0)
+        result[local, 1] = acc_k[...].astype(jnp.bfloat16)
+        result[local, 2] = acc_v[...].astype(jnp.bfloat16)
+
+        def reply(turn, carry, local=local):
+            back_copy(local, turn).start()
+            return carry
+
+        lax.fori_loop(0, group - 1, reply, 0)
+
+    def finish(head, got_q, got_k, got_v, carry):
+        at = columns(head)
+        sums = []
+        for ref, out, gain, got in ((q_ref, out_q, gain_q, got_q), (k_ref, out_k, gain_k, got_k)):
+            states = ref[:, at].astype(jnp.float32)
+            inverse = inverse_of(states)
+            unit = states * inverse
+            grad_hat = got.astype(jnp.float32)
+            scaled = grad_hat * gain
+            inner = jnp.mean(scaled * unit, -1, keepdims=True)
+            out[:, at] = (inverse * (scaled - unit * inner)).astype(jnp.bfloat16)
+            sums.append(jnp.sum((grad_hat * unit).reshape(tokens // 8, 8, 128), axis=0))
+        out_v[:, at] = got_v
+        return (carry[0] + sums[0], carry[1] + sums[1])
+
+    nothing = jnp.zeros((8, 128), jnp.float32)
+    terms = (nothing, nothing)
+    for local in range(local_heads):
+        terms = finish(
+            me * local_heads + local,
+            result[local, 0, rows(me), :],
+            result[local, 1, rows(me), :],
+            result[local, 2, rows(me), :],
+            terms,
+        )
+
+        def collect(turn, carry, local=local):
+            source = (me + group - offset(turn)) % group
+            back_arrival(local, turn).wait_recv()
+            return finish(
+                source * local_heads + local,
+                back[local, source, 0],
+                back[local, source, 1],
+                back[local, source, 2],
+                carry,
+            )
+
+        terms = lax.fori_loop(0, group - 1, collect, terms)
+
+    first = lax.broadcasted_iota(jnp.int32, (8, 128), 0) == 0
+    both = jnp.where(
+        first,
+        jnp.sum(terms[0], 0, keepdims=True),
+        jnp.sum(terms[1], 0, keepdims=True),
+    )
+    gains[...] = both
+    gain_held[me_all] = both
+
+    def gain_copy(step, sign):
+        other = (me_all + everyone + sign * step) % everyone
+        slot = me_all if sign > 0 else other
+        return pltpu.make_async_remote_copy(
+            src_ref=gains,
+            dst_ref=gain_held.at[slot],
+            send_sem=gain_send.at[step],
+            recv_sem=gain_recv.at[step],
+            device_id=place_all(other),
+            device_id_type=MESH,
+        )
+
+    def gain_start(step, carry):
+        gain_copy(step, 1).start()
+        return carry
+
+    def gain_wait(step, carry):
+        gain_copy(step, -1).wait_recv()
+        gain_copy(step, 1).wait_send()
+        return carry
+
+    lax.fori_loop(1, everyone, gain_start, 0)
+    for local in range(local_heads):
+
+        def drain(turn, carry, local=local):
+            send_copy(local, turn).wait_send()
+            back_copy(local, turn).wait_send()
+            return carry
+
+        lax.fori_loop(0, group - 1, drain, 0)
+    lax.fori_loop(1, everyone, gain_wait, 0)
+    summed = jnp.sum(gain_held[...], axis=0)
+    total_q[...] = summed[0:1]
+    total_k[...] = summed[1:2]
+
+
+def on_device_fused(
+    queries, key_states, value_states, grad_output, gain_query, gain_key, block_keys, block_counts
+):
+    tokens, features = queries.shape[1:]
+    heads = features // gain_query.shape[0]
+    group = lax.axis_size(("seq", "pair"))
+    replicas = lax.axis_size("dp")
+    local_heads = heads // group
+    seq_len = tokens * group
+    everyone = group * replicas
+    low = jnp.bfloat16
+    vmem = pl.BlockSpec(memory_space=pltpu.VMEM)
+    smem = pl.BlockSpec(memory_space=pltpu.SMEM)
+    shape = jax.ShapeDtypeStruct((tokens, features), low)
+    line = jax.ShapeDtypeStruct((1, 128), jnp.float32)
+    dma = pltpu.SemaphoreType.DMA
+    outs = pl.pallas_call(
+        functools.partial(
+            fused_kernel, (lax.axis_size("pair"), group, replicas, local_heads)
+        ),
+        out_shape=(shape, shape, shape, line, line),
+        in_specs=[vmem] * 6 + [smem] * 2,
+        out_specs=(vmem,) * 5,
+        scratch_shapes=[
+            pltpu.VMEM((local_heads, group, 4, tokens, 128), low),
+            pltpu.VMEM((local_heads, 4, seq_len, 128), low),
+            pltpu.VMEM((seq_len // CHUNK, seq_len, CHUNK), jnp.float32),
+            pltpu.VMEM((seq_len, 128), jnp.float32),
+            pltpu.VMEM((seq_len, 128), jnp.float32),
+            pltpu.VMEM((2, 128, seq_len), low),
+            pltpu.VMEM((local_heads, 3, seq_len, 128), low),
+            pltpu.VMEM((local_heads, group, 3, tokens, 128), low),
+            pltpu.VMEM((8, 128), jnp.float32),
+            pltpu.VMEM((everyone, 8, 128), jnp.float32),
+            dma((local_heads, group)),
+            dma((local_heads, group)),
+            dma((local_heads, group)),
+            dma((local_heads, group)),
+            dma((everyone,)),
+            dma((everyone,)),
+        ],
+        compiler_params=pltpu.CompilerParams(
+            collective_id=0, has_side_effects=True, vmem_limit_bytes=56 * 1024 * 1024
+        ),
+    )(
+        queries[0], key_states[0], value_states[0], grad_output[0],
+        gain_query.reshape(1, 128), gain_key.reshape(1, 128), block_keys, block_counts,
+    )
+    return (
+        outs[0][None], outs[1][None], outs[2][None], outs[3].reshape(128), outs[4].reshape(128)
+    )
+
+
+def on_device_any(*operands):
+    queries, gain_query = operands[0], operands[4]
+    tokens, features = queries.shape[1:]
+    group = lax.axis_size(("seq", "pair"))
+    heads = features // gain_query.shape[0]
+    fits = group > 1 and group % 2 == 0 and heads % group == 0 and tokens % BLOCK == 0
+    if fits and gain_query.shape[0] == 128 and tokens * group <= 1024:
+        return on_device_fused(*operands)
+    return on_device(*operands)
+
+
 def solution(mesh):
     placed = (
         P(("groups", "dp"), ("seq", "pair"), None),
@@ -214,7 +555,7 @@
         P(),
     )
     return jax.shard_map(
-        on_device,
+        on_device_any,
         mesh=mesh,
         in_specs=placed,
         out_specs=(

time: 241 us -> 102 us (0.42)
  Pallas kernels: 0 us -> 94.9 us
  waiting for transfers between devices: 90.8 us -> 0 us
  local copies, waits for them, and re-layouts: 40 us -> 6.49 us
  blocking collectives: 31.8 us -> 0 us
  starting transfers between devices: 29.5 us -> 0 us
  other arithmetic: 27.7 us -> 0 us
  matrix products: 18.7 us -> 0 us
    pallas_call x0 -> x1, Pallas kernels: none -> 94.9 us  [on_device_fused(): pl.pallas_call(functools.partial(fused_kernel, (lax.axis_size('pair'), gr...]
    all_to_all x7 -> x0, waiting for transfers between devices: 90.8 us -> none  [the longest x1 15.4 us: on_device(): lax.all_to_all(key_copies(value_rows, row_parts), ('seq', 'pair'), split_...]
    psum x1 -> x0, blocking collectives: 31.8 us -> none  [on_device(): lax.psum((query_term, key_term), ('seq', 'dp', 'pair'))]
    all_to_all x7 -> x0, starting transfers between devices: 29.5 us -> none  [the longest x1 6.46 us: on_device(): lax.all_to_all(to_items(query_hat, row_parts), ('seq', 'pair'), split_axi...]
    scatter-add x8 -> x0, other arithmetic: 20.7 us -> none  [the longest x4 13.8 us: one_group(): grad_values = grad_values.at[head_at, chosen].add(value_terms)]
    dot_general x20 -> x0, matrix products: 13.1 us -> none  [the longest x4 5 us: one_group(): jnp.einsum('nqk,nqd->nkd', d_scores, query_block, preferred_element_type=...]
    dynamic_slice x28 -> x0, local copies, waits for them, and re-layouts: 10.7 us -> none  [the longest x8 5.01 us: one_group(): lax.dynamic_index_in_dim(value_full, head_at, 0, False)]
    gather x16 -> x0, local copies, waits for them, and re-layouts: 8.17 us -> none  [the longest x8 2.97 us: one_group(): jnp.take(block_counts, chosen).reshape(group_blocks, key_slots, 1)]
  transfers between devices with their start and end apart: 7 -> 0, of which waited for: 7 -> 0; matrix products, arithmetic and copies ran while one was open for 6% -> 0% of each run, Pallas kernels for 0% -> 0%
where the time goes in v1:
time: 102 us
  Pallas kernels  94.9 us (93%)
  local copies, waits for them, and re-layouts  6.49 us (6%)
    pallas_call x1, Pallas kernels, on_device_fused(): pl.pallas_call(functools.partial(fused_kernel, (lax.axis_size('pair'), gr...  94.9 us
    unnamed x16, local copies, waits for them, and re-layouts  6.49 us

profile of v1, /device:TPU:0, one launch (start us, length us, event | category | flops | bytes accessed | tf_op | source)
XLA Modules:
  0.0 102.0 jit_solution(17667413140462773313)
XLA Ops:
  0.6 0.0 copy-start.2
  0.6 0.7 copy-done.2
  1.3 0.7 copy.13.keys_ref
  2.0 94.9 %shard_map.119 = (bf16[128,2048]{1,0:T(8,128)(2,1)}, bf16[128,2048]{1,0:T(8,128)(2,1)}, bf16[128,2048]{1,0:T(8,128)(2,1)}, f32[1,128]{1,0:T(1,128)}, f32[1,128]{1,0:T(1,128)}) custom-call(bf16[128,2048]{1,0:T(8,128)(2,1)} %bitcast.14, bf16[128,2048]{1,0:T(8,128)(2,1)} %bitcast.15, bf16[128,2048]{1,0:T(8,128)(2,1)} %bitcast.16, bf16[128,2048]{1,0:T(8,128)(2,1)} %bitcast.17, ...), custom_call_target="tpu_custom_call" | custom-call | tf_op jit(solution)/shard_map/pallas_call | solution.py:498
  96.9 0.0 copy-start.1
  96.9 1.9 %copy.19 = bf16[1,128,2048]{2,1,0:T(8,128)(2,1)} copy(bf16[1,128,2048]{2,1,0:T(8,128)(2,1)} %bitcast.13) | data formatting | bytes 1048576
  98.8 0.0 copy-done.1
  98.8 0.0 copy-start
  98.8 0.8 copy.20
  99.6 0.4 copy-done
  100.0 0.0 copy-start.4
  100.0 0.8 copy.21
  100.8 0.0 copy-done.4
  100.8 0.0 copy-start.3
  100.8 0.5 copy.22
  101.3 0.2 copy-done.3
  101.5 0.5 copy.23
Async XLA Ops:
  0.6 0.7 copy-start.2
  96.9 2.0 %copy-start.1 = (bf16[128,2048]{1,0:T(8,128)(2,1)S(1)}, bf16[128,2048]{1,0:T(8,128)(2,1)}, u32[]{:S(2)}) copy-start(bf16[128,2048]{1,0:T(8,128)(2,1)} %get-tuple-element.11) | copy-start | bytes 1572868
  98.8 1.2 %copy-start = (bf16[128,2048]{1,0:T(8,128)(2,1)S(1)}, bf16[128,2048]{1,0:T(8,128)(2,1)}, u32[]{:S(2)}) copy-start(bf16[128,2048]{1,0:T(8,128)(2,1)} %get-tuple-element.12) | copy-start | bytes 1572868
  100.0 0.8 copy-start.4
  100.8 0.7 copy-start.3

commit v2 on v1

--- a/solution.py
+++ b/solution.py
@@ -222,15 +222,16 @@
 
 def fused_kernel(
     sizes,
-    q_ref, k_ref, v_ref, g_ref, gain_q_ref, gain_k_ref, keys_ref, counts_ref,
-    out_q, out_k, out_v, total_q, total_k,
+    q_in, k_in, v_in, g_in, gain_q_ref, gain_k_ref, keys_in, counts_in,
+    out_q, out_k, out_v, totals,
+    q_ref, k_ref, v_ref, g_ref, keys_ref, counts_ref,
     sent, held, bias, acc_k, acc_v, flipped, result, back, gains, gain_held,
-    sent_send, sent_recv, result_send, result_recv, gain_send, gain_recv,
+    sent_send, sent_recv, result_send, result_recv, gain_send, gain_recv, load_sem,
 ):
     pairs, group, replicas, local_heads = sizes
     tokens = q_ref.shape[0]
     seq_len = held.shape[2]
-    total_blocks, slots = keys_ref.shape
+    slots, total_blocks = keys_ref.shape
     everyone = group * replicas
     me = lax.axis_index("seq") * pairs + lax.axis_index("pair")
     me_all = lax.axis_index("dp") * group + me
@@ -242,14 +243,34 @@
         inside = index % group
         return {"dp": index // group, "seq": inside // pairs, "pair": inside % pairs}
 
-    def offset(turn):
-        return group // 2 + ((turn + 1) // 2) * (1 - 2 * (turn % 2))
-
+    def peer_of(turn):
+        half = group // 2
+        late = turn // half
+        mask = (1 - late) * (half + turn) + late * (group - 1 - turn)
+        peer, bit = 0, 1
+        while bit < group:
+            peer += ((me // bit + mask // bit) % 2) * bit
+            bit *= 2
+        return peer
+
+    loads = [
+        pltpu.make_async_copy(source, target, load_sem.at[at])
+        for at, (source, target) in enumerate(
+            (
+                (q_in, q_ref), (k_in, k_ref), (v_in, v_ref), (g_in, g_ref),
+                (keys_in, keys_ref), (counts_in, counts_ref),
+            )
+        )
+    ]
+    for load in loads:
+        load.start()
     barrier = pltpu.get_barrier_semaphore()
     for step in range(1, everyone):
         pl.semaphore_signal(
             barrier, inc=1, device_id=place_all((me_all + step) % everyone), device_id_type=MESH
         )
+    for load in loads:
+        load.wait()
     gain_q = gain_q_ref[...]
     gain_k = gain_k_ref[...]
 
@@ -267,7 +288,7 @@
         return (states * inverse_of(states) * gain).astype(jnp.bfloat16)
 
     def send_copy(local, turn):
-        peer = (me + offset(turn)) % group
+        peer = peer_of(turn)
         return pltpu.make_async_remote_copy(
             src_ref=sent.at[local, peer],
             dst_ref=held.at[local, :, rows(me), :],
@@ -278,7 +299,7 @@
         )
 
     def arrival(local, turn):
-        source = (me + group - offset(turn)) % group
+        source = peer_of(turn)
         return pltpu.make_async_remote_copy(
             src_ref=sent.at[local, source],
             dst_ref=held.at[local, :, rows(source), :],
@@ -289,7 +310,7 @@
         )
 
     def back_copy(local, turn):
-        peer = (me + offset(turn)) % group
+        peer = peer_of(turn)
         return pltpu.make_async_remote_copy(
             src_ref=result.at[local, :, rows(peer), :],
             dst_ref=back.at[local, me],
@@ -300,7 +321,7 @@
         )
 
     def back_arrival(local, turn):
-        source = (me + group - offset(turn)) % group
+        source = peer_of(turn)
         return pltpu.make_async_remote_copy(
             src_ref=result.at[local, :, rows(source), :],
             dst_ref=back.at[local, source],
@@ -313,7 +334,7 @@
     for local in range(local_heads):
 
         def prepare(turn, carry, local=local):
-            peer = (me + offset(turn)) % group
+            peer = peer_of(turn)
             at = columns(peer * local_heads + local)
             sent[local, peer, 0] = hat(q_ref[:, at], gain_q)
             sent[local, peer, 1] = hat(k_ref[:, at], gain_k)
@@ -344,15 +365,16 @@
     for block in range(total_blocks):
         chunk, side = block // (CHUNK // BLOCK), block % (CHUNK // BLOCK)
         for other in range(total_blocks):
-            live = counts_ref[other]
-            limit = jnp.int32(0)
+            live = counts_ref[0:1, other : other + 1]
+            limit = jnp.zeros_like(live)
             for slot in range(slots):
-                limit = jnp.where(keys_ref[block, slot] == other, live, limit)
+                limit = jnp.where(keys_ref[slot : slot + 1, block : block + 1] == other, live, limit)
             bias[
                 chunk, other * BLOCK : (other + 1) * BLOCK, side * BLOCK : (side + 1) * BLOCK
             ] = jnp.where(place_in < limit, 0.0, -1e30)
 
     scale = 1.0 / math.sqrt(128)
+    gain_sums = [jnp.zeros((8, 128), jnp.float32), jnp.zeros((8, 128), jnp.float32)]
     for local in range(local_heads):
 
         def landed(turn, carry, local=local):
@@ -389,56 +411,32 @@
         result[local, 1] = acc_k[...].astype(jnp.bfloat16)
         result[local, 2] = acc_v[...].astype(jnp.bfloat16)
 
+        def fold(at, carry, local=local):
+            part = pl.ds(pl.multiple_of(at * BLOCK, BLOCK), BLOCK)
+            return tuple(
+                total
+                + jnp.sum(
+                    (
+                        result[local, which, part, :].astype(jnp.float32)
+                        * held[local, which, part, :].astype(jnp.float32)
+                    ).reshape(BLOCK // 8, 8, 128),
+                    axis=0,
+                )
+                for which, total in enumerate(carry)
+            )
+
         def reply(turn, carry, local=local):
             back_copy(local, turn).start()
             return carry
 
         lax.fori_loop(0, group - 1, reply, 0)
-
-    def finish(head, got_q, got_k, got_v, carry):
-        at = columns(head)
-        sums = []
-        for ref, out, gain, got in ((q_ref, out_q, gain_q, got_q), (k_ref, out_k, gain_k, got_k)):
-            states = ref[:, at].astype(jnp.float32)
-            inverse = inverse_of(states)
-            unit = states * inverse
-            grad_hat = got.astype(jnp.float32)
-            scaled = grad_hat * gain
-            inner = jnp.mean(scaled * unit, -1, keepdims=True)
-            out[:, at] = (inverse * (scaled - unit * inner)).astype(jnp.bfloat16)
-            sums.append(jnp.sum((grad_hat * unit).reshape(tokens // 8, 8, 128), axis=0))
-        out_v[:, at] = got_v
-        return (carry[0] + sums[0], carry[1] + sums[1])
-
-    nothing = jnp.zeros((8, 128), jnp.float32)
-    terms = (nothing, nothing)
-    for local in range(local_heads):
-        terms = finish(
-            me * local_heads + local,
-            result[local, 0, rows(me), :],
-            result[local, 1, rows(me), :],
-            result[local, 2, rows(me), :],
-            terms,
-        )
-
-        def collect(turn, carry, local=local):
-            source = (me + group - offset(turn)) % group
-            back_arrival(local, turn).wait_recv()
-            return finish(
-                source * local_heads + local,
-                back[local, source, 0],
-                back[local, source, 1],
-                back[local, source, 2],
-                carry,
-            )
-
-        terms = lax.fori_loop(0, group - 1, collect, terms)
+        gain_sums = lax.fori_loop(0, total_blocks, fold, tuple(gain_sums))
 
     first = lax.broadcasted_iota(jnp.int32, (8, 128), 0) == 0
     both = jnp.where(
         first,
-        jnp.sum(terms[0], 0, keepdims=True),
-        jnp.sum(terms[1], 0, keepdims=True),
+        jnp.sum(gain_sums[0], 0, keepdims=True) / gain_q,
+        jnp.sum(gain_sums[1], 0, keepdims=True) / gain_k,
     )
     gains[...] = both
     gain_held[me_all] = both
@@ -465,6 +463,40 @@
         return carry
 
     lax.fori_loop(1, everyone, gain_start, 0)
+
+    def finish(head, got_q, got_k, got_v):
+        at = columns(head)
+        for ref, out, gain, got in ((q_ref, out_q, gain_q, got_q), (k_ref, out_k, gain_k, got_k)):
+            states = ref[:, at].astype(jnp.float32)
+            inverse = inverse_of(states)
+            unit = states * inverse
+            grad_hat = got.astype(jnp.float32)
+            scaled = grad_hat * gain
+            inner = jnp.mean(scaled * unit, -1, keepdims=True)
+            out[:, at] = (inverse * (scaled - unit * inner)).astype(jnp.bfloat16)
+        out_v[:, at] = got_v
+
+    for local in range(local_heads):
+        finish(
+            me * local_heads + local,
+            result[local, 0, rows(me), :],
+            result[local, 1, rows(me), :],
+            result[local, 2, rows(me), :],
+        )
+
+        def collect(turn, carry, local=local):
+            source = peer_of(turn)
+            back_arrival(local, turn).wait_recv()
+            finish(
+                source * local_heads + local,
+                back[local, source, 0],
+                back[local, source, 1],
+                back[local, source, 2],
+            )
+            return carry
+
+        lax.fori_loop(0, group - 1, collect, 0)
+
     for local in range(local_heads):
 
         def drain(turn, carry, local=local):
@@ -474,9 +506,24 @@
 
         lax.fori_loop(0, group - 1, drain, 0)
     lax.fori_loop(1, everyone, gain_wait, 0)
-    summed = jnp.sum(gain_held[...], axis=0)
-    total_q[...] = summed[0:1]
-    total_k[...] = summed[1:2]
+    totals[...] = jnp.sum(gain_held[...], axis=0)
+
+
+def place_kernel(
+    a_in, b_in, c_in, totals, a_out, b_out, c_out, total_q, total_k, a_mid, b_mid, c_mid, sem
+):
+    steps = ((a_in, a_mid, a_out), (b_in, b_mid, b_out), (c_in, c_mid, c_out))
+    first = [pltpu.make_async_copy(i, m, sem.at[0, at]) for at, (i, m, _) in enumerate(steps)]
+    second = [pltpu.make_async_copy(m, o, sem.at[1, at]) for at, (_, m, o) in enumerate(steps)]
+    for move in first:
+        move.start()
+    total_q[...] = totals[0:1]
+    total_k[...] = totals[1:2]
+    for before, after in zip(first, second):
+        before.wait()
+        after.start()
+    for move in second:
+        move.wait()
 
 
 def on_device_fused(
@@ -491,7 +538,7 @@
     everyone = group * replicas
     low = jnp.bfloat16
     vmem = pl.BlockSpec(memory_space=pltpu.VMEM)
-    smem = pl.BlockSpec(memory_space=pltpu.SMEM)
+    hbm = pl.BlockSpec(memory_space=pl.ANY)
     shape = jax.ShapeDtypeStruct((tokens, features), low)
     line = jax.ShapeDtypeStruct((1, 128), jnp.float32)
     dma = pltpu.SemaphoreType.DMA
@@ -499,10 +546,16 @@
         functools.partial(
             fused_kernel, (lax.axis_size("pair"), group, replicas, local_heads)
         ),
-        out_shape=(shape, shape, shape, line, line),
-        in_specs=[vmem] * 6 + [smem] * 2,
-        out_specs=(vmem,) * 5,
+        out_shape=(shape, shape, shape, jax.ShapeDtypeStruct((8, 128), jnp.float32)),
+        in_specs=[hbm] * 4 + [vmem] * 2 + [hbm] * 2,
+        out_specs=(vmem,) * 4,
         scratch_shapes=[
+            pltpu.VMEM((tokens, features), low),
+            pltpu.VMEM((tokens, features), low),
+            pltpu.VMEM((tokens, features), low),
+            pltpu.VMEM((tokens, features), low),
+            pltpu.VMEM(block_keys.shape[::-1], block_keys.dtype),
+            pltpu.VMEM((1, block_counts.shape[0]), block_counts.dtype),
             pltpu.VMEM((local_heads, group, 4, tokens, 128), low),
             pltpu.VMEM((local_heads, 4, seq_len, 128), low),
             pltpu.VMEM((seq_len // CHUNK, seq_len, CHUNK), jnp.float32),
@@ -519,14 +572,22 @@
             dma((local_heads, group)),
             dma((everyone,)),
             dma((everyone,)),
+            dma((6,)),
         ],
         compiler_params=pltpu.CompilerParams(
             collective_id=0, has_side_effects=True, vmem_limit_bytes=56 * 1024 * 1024
         ),
     )(
         queries[0], key_states[0], value_states[0], grad_output[0],
-        gain_query.reshape(1, 128), gain_key.reshape(1, 128), block_keys, block_counts,
-    )
+        gain_query.reshape(1, 128), gain_key.reshape(1, 128), block_keys.T, block_counts.reshape(1, -1),
+    )
+    outs = pl.pallas_call(
+        place_kernel,
+        out_shape=(shape, shape, shape, line, line),
+        in_specs=[hbm] * 3 + [vmem],
+        out_specs=(hbm,) * 3 + (vmem,) * 2,
+        scratch_shapes=[pltpu.VMEM((tokens, features), low)] * 3 + [dma((2, 3))],
+    )(*outs)
     return (
         outs[0][None], outs[1][None], outs[2][None], outs[3].reshape(128), outs[4].reshape(128)
     )

time: 102 us -> 94.6 us (0.927)
  local copies, waits for them, and re-layouts: 6.49 us -> 0 us
  Pallas kernels: 94.9 us -> 93.8 us
    unnamed x16 -> x0, local copies, waits for them, and re-layouts: 6.49 us -> none
    pallas_call x1, Pallas kernels: 94.9 us -> 90.4 us  [on_device_fused(): pl.pallas_call(functools.partial(fused_kernel, (lax.axis_size('pair'), gr...]
    pallas_call x0 -> x1, Pallas kernels: none -> 3.42 us  [on_device_fused(): pl.pallas_call(place_kernel, out_shape=(shape, shape, shape, line, line),...]
where the time goes in v2:
time: 94.6 us; the launch traced here: 94.4 us
  Pallas kernels  93.8 us (99%)
    pallas_call x1, Pallas kernels, on_device_fused(): pl.pallas_call(functools.partial(fused_kernel, (lax.axis_size('pair'), gr...  90.4 us
    pallas_call x1, Pallas kernels, on_device_fused(): pl.pallas_call(place_kernel, out_shape=(shape, shape, shape, line, line),...  3.42 us

profile of v2, /device:TPU:0, one launch (start us, length us, event | category | flops | bytes accessed | tf_op | source)
XLA Modules:
  0.0 94.4 jit_solution(12937352688620341321)
XLA Ops:
  0.6 90.4 %shard_map.119 = (bf16[128,2048]{1,0:T(8,128)(2,1)}, bf16[128,2048]{1,0:T(8,128)(2,1)}, bf16[128,2048]{1,0:T(8,128)(2,1)}, f32[8,128]{1,0:T(8,128)}) custom-call(bf16[128,2048]{1,0:T(8,128)(2,1)} %bitcast.13, bf16[128,2048]{1,0:T(8,128)(2,1)} %bitcast.14, bf16[128,2048]{1,0:T(8,128)(2,1)} %bitcast.15, bf16[128,2048]{1,0:T(8,128)(2,1)} %bitcast.16, ...), custom_call_target="tpu_custom_call" | custom-call | tf_op jit(solution)/shard_map/pallas_call | solution.py:545
  91.0 3.4 %shard_map.120 = (bf16[128,2048]{1,0:T(8,128)(2,1)}, bf16[128,2048]{1,0:T(8,128)(2,1)}, bf16[128,2048]{1,0:T(8,128)(2,1)}, f32[1,128]{1,0:T(1,128)}, f32[1,128]{1,0:T(1,128)}) custom-call(bf16[128,2048]{1,0:T(8,128)(2,1)} %get-tuple-element.14.a_in, bf16[128,2048]{1,0:T(8,128)(2,1)} %get-tuple-element.15.b_in, bf16[128,2048]{1,0:T(8,128)(2,1)} %get-tuple-element.16.c_in, ...), custom_call_target="tpu_custom_call" | custom-call | tf_op jit(solution)/shard_map/pallas_call | solution.py:584

commit v3 on v2

--- a/solution.py
+++ b/solution.py
@@ -224,7 +224,7 @@
     sizes,
     q_in, k_in, v_in, g_in, gain_q_ref, gain_k_ref, keys_in, counts_in,
     out_q, out_k, out_v, totals,
-    q_ref, k_ref, v_ref, g_ref, keys_ref, counts_ref,
+    q_ref, k_ref, v_ref, g_ref, keys_ref, counts_ref, units, inverses,
     sent, held, bias, acc_k, acc_v, flipped, result, back, gains, gain_held,
     sent_send, sent_recv, result_send, result_recv, gain_send, gain_recv, load_sem,
 ):
@@ -372,6 +372,47 @@
             bias[
                 chunk, other * BLOCK : (other + 1) * BLOCK, side * BLOCK : (side + 1) * BLOCK
             ] = jnp.where(place_in < limit, 0.0, -1e30)
+
+    def remember(head, carry):
+        for which, ref in enumerate((q_ref, k_ref)):
+            states = ref[:, columns(head)].astype(jnp.float32)
+            inverse = inverse_of(states)
+            units[which, head] = states * inverse
+            inverses[which, head] = jnp.broadcast_to(inverse, states.shape)
+        return carry
+
+    lax.fori_loop(0, local_heads * group, remember, 0)
+    def gain_copy(step, sign):
+        other = (me_all + everyone + sign * step) % everyone
+        slot = me_all if sign > 0 else other
+        return pltpu.make_async_remote_copy(
+            src_ref=gains,
+            dst_ref=gain_held.at[slot],
+            send_sem=gain_send.at[step],
+            recv_sem=gain_recv.at[step],
+            device_id=place_all(other),
+            device_id_type=MESH,
+        )
+
+    def gain_start(step, carry):
+        gain_copy(step, 1).start()
+        return carry
+
+    def gain_wait(step, carry):
+        gain_copy(step, -1).wait_recv()
+        gain_copy(step, 1).wait_send()
+        return carry
+
+    def share_gains(gain_sums):
+        first = lax.broadcasted_iota(jnp.int32, (8, 128), 0) == 0
+        both = jnp.where(
+            first,
+            jnp.sum(gain_sums[0], 0, keepdims=True) / gain_q,
+            jnp.sum(gain_sums[1], 0, keepdims=True) / gain_k,
+        )
+        gains[...] = both
+        gain_held[me_all] = both
+        lax.fori_loop(1, everyone, gain_start, 0)
 
     scale = 1.0 / math.sqrt(128)
     gain_sums = [jnp.zeros((8, 128), jnp.float32), jnp.zeros((8, 128), jnp.float32)]
@@ -429,47 +470,16 @@
             back_copy(local, turn).start()
             return carry
 
+        gain_sums = lax.fori_loop(0, total_blocks, fold, tuple(gain_sums))
+        if local == local_heads - 1:
+            share_gains(gain_sums)
         lax.fori_loop(0, group - 1, reply, 0)
-        gain_sums = lax.fori_loop(0, total_blocks, fold, tuple(gain_sums))
-
-    first = lax.broadcasted_iota(jnp.int32, (8, 128), 0) == 0
-    both = jnp.where(
-        first,
-        jnp.sum(gain_sums[0], 0, keepdims=True) / gain_q,
-        jnp.sum(gain_sums[1], 0, keepdims=True) / gain_k,
-    )
-    gains[...] = both
-    gain_held[me_all] = both
-
-    def gain_copy(step, sign):
-        other = (me_all + everyone + sign * step) % everyone
-        slot = me_all if sign > 0 else other
-        return pltpu.make_async_remote_copy(
-            src_ref=gains,
-            dst_ref=gain_held.at[slot],
-            send_sem=gain_send.at[step],
-            recv_sem=gain_recv.at[step],
-            device_id=place_all(other),
-            device_id_type=MESH,
-        )
-
-    def gain_start(step, carry):
-        gain_copy(step, 1).start()
-        return carry
-
-    def gain_wait(step, carry):
-        gain_copy(step, -1).wait_recv()
-        gain_copy(step, 1).wait_send()
-        return carry
-
-    lax.fori_loop(1, everyone, gain_start, 0)
 
     def finish(head, got_q, got_k, got_v):
         at = columns(head)
-        for ref, out, gain, got in ((q_ref, out_q, gain_q, got_q), (k_ref, out_k, gain_k, got_k)):
-            states = ref[:, at].astype(jnp.float32)
-            inverse = inverse_of(states)
-            unit = states * inverse
+        for which, (out, gain, got) in enumerate(((out_q, gain_q, got_q), (out_k, gain_k, got_k))):
+            unit = units[which, head]
+            inverse = inverses[which, head]
             grad_hat = got.astype(jnp.float32)
             scaled = grad_hat * gain
             inner = jnp.mean(scaled * unit, -1, keepdims=True)
@@ -484,7 +494,14 @@
             result[local, 2, rows(me), :],
         )
 
-        def collect(turn, carry, local=local):
+        def drain(turn, carry, local=local):
+            send_copy(local, turn).wait_send()
+            return carry
+
+        lax.fori_loop(0, group - 1, drain, 0)
+
+        def collect(step, carry, local=local):
+            turn = group - 2 - step
             source = peer_of(turn)
             back_arrival(local, turn).wait_recv()
             finish(
@@ -495,18 +512,18 @@
             )
             return carry
 
+        if local == local_heads - 1:
+            lax.fori_loop(1, everyone, gain_wait, 0)
+            totals[...] = jnp.sum(gain_held[...], axis=0)
         lax.fori_loop(0, group - 1, collect, 0)
 
     for local in range(local_heads):
 
-        def drain(turn, carry, local=local):
-            send_copy(local, turn).wait_send()
+        def replied(turn, carry, local=local):
             back_copy(local, turn).wait_send()
             return carry
 
-        lax.fori_loop(0, group - 1, drain, 0)
-    lax.fori_loop(1, everyone, gain_wait, 0)
-    totals[...] = jnp.sum(gain_held[...], axis=0)
+        lax.fori_loop(0, group - 1, replied, 0)
 
 
 def place_kernel(
@@ -556,6 +573,8 @@
             pltpu.VMEM((tokens, features), low),
             pltpu.VMEM(block_keys.shape[::-1], block_keys.dtype),
             pltpu.VMEM((1, block_counts.shape[0]), block_counts.dtype),
+            pltpu.VMEM((2, heads, tokens, 128), jnp.float32),
+            pltpu.VMEM((2, heads, tokens, 128), jnp.float32),
             pltpu.VMEM((local_heads, group, 4, tokens, 128), low),
             pltpu.VMEM((local_heads, 4, seq_len, 128), low),
             pltpu.VMEM((seq_len // CHUNK, seq_len, CHUNK), jnp.float32),

time: 94.6 us -> 93.1 us (0.984)
  the two profiles are of different devices: /device:TPU:0 before, /device:TPU:9 now
where the time goes in v3:
time: 93.1 us; the launch traced here: 92.9 us
  Pallas kernels  92.2 us (99%)
    pallas_call x1, Pallas kernels, on_device_fused(): pl.pallas_call(functools.partial(fused_kernel, (lax.axis_size('pair'), gr...  88.8 us
    pallas_call x1, Pallas kernels, on_device_fused(): pl.pallas_call(place_kernel, out_shape=(shape, shape, shape, line, line),...  3.42 us

profile of v3, /device:TPU:9, one launch (start us, length us, event | category | flops | bytes accessed | tf_op | source)
XLA Modules:
  0.0 92.9 jit_solution(13153283805439094591)
XLA Ops:
  0.6 88.8 %shard_map.119 = (bf16[128,2048]{1,0:T(8,128)(2,1)}, bf16[128,2048]{1,0:T(8,128)(2,1)}, bf16[128,2048]{1,0:T(8,128)(2,1)}, f32[8,128]{1,0:T(8,128)}) custom-call(bf16[128,2048]{1,0:T(8,128)(2,1)} %bitcast.13, bf16[128,2048]{1,0:T(8,128)(2,1)} %bitcast.14, bf16[128,2048]{1,0:T(8,128)(2,1)} %bitcast.15, bf16[128,2048]{1,0:T(8,128)(2,1)} %bitcast.16, ...), custom_call_target="tpu_custom_call" | custom-call | tf_op jit(solution)/shard_map/pallas_call | solution.py:562
  89.5 3.4 %shard_map.120 = (bf16[128,2048]{1,0:T(8,128)(2,1)}, bf16[128,2048]{1,0:T(8,128)(2,1)}, bf16[128,2048]{1,0:T(8,128)(2,1)}, f32[1,128]{1,0:T(1,128)}, f32[1,128]{1,0:T(1,128)}) custom-call(bf16[128,2048]{1,0:T(8,128)(2,1)} %get-tuple-element.14.a_in, bf16[128,2048]{1,0:T(8,128)(2,1)} %get-tuple-element.15.b_in, bf16[128,2048]{1,0:T(8,128)(2,1)} %get-tuple-element.16.c_in, ...), custom_call_target="tpu_custom_call" | custom-call | tf_op jit(solution)/shard_map/pallas_call | solution.py:603
